TPU v7x, 32 devices: a whole 2x2x4 slice. The times are simulated.
32 devices in a mesh: row: 8 (over z, core), col: 4 (over y, x).
Axes of the slice: x: 2, y: 2, z: 4, core: 2. Of those that a mesh axis runs over, the one named last changes fastest.
Arguments:
- hidden_pre: bfloat16 [512, 16384], P('col', 'row'), may hold values from -6 to 6
- weight_blocks: bfloat16 [8, 4, 8, 256, 256], P('row', 'col'), may hold values from -0.09375 to 0.09375
- block_rows: int32 [8, 4, 8], P('row', 'col'), may hold values from 0 to 63, as said below
- block_cols: int32 [8, 4, 8], P('row', 'col'), may hold values from 0 to 31, as said below
- block_counts: int32 [8, 4], P('row', 'col'), may hold values from 2 to 8, as said below
- out_grad: bfloat16 [512, 8192], P('row', 'col'), may hold values from -6 to 6
Outputs:
- projected: bfloat16 [512, 8192], P('row', 'col')
- grad_hidden: bfloat16 [512, 16384], P('col', 'row')
- grad_blocks: float32 [8, 4, 8, 256, 256], P('row', 'col')
Inputs may be any that keep to these rules, and one draw needn't show every extreme that they name: `block_rows`: owner (r, c) holds only blocks of block-rows r * 8 to (r + 1) * 8 - 1 and block-columns c * 8 to (c + 1) * 8 - 1; the 8 slots of one owner name 8 different blocks. `block_cols`: same owner ranges as block_rows. `block_counts`: some owner holds exactly 8 live blocks and some owner exactly 2.
All inputs are finite; a program needn't handle non-finite values.
Results may differ from a plain program's by a relative error of at most 0.0051.
Values may be sent and summed in bfloat16 or wider, within the bound.
A program may use at most 128 MiB of HBM per device.

v0:
```python
import jax
import jax.numpy as jnp
from jax import lax
from jax.sharding import PartitionSpec as P


def silu_rounded(values):
    return jax.nn.silu(values.astype(jnp.float32)).astype(jnp.bfloat16)


def on_device(hidden_pre, weight_blocks, block_rows, block_cols, block_counts, out_grad):
    width = weight_blocks.shape[-1]
    slot_count = weight_blocks.shape[2]
    row_span = hidden_pre.shape[1] // width
    col_span = out_grad.shape[1] // width
    row_base = lax.axis_index("row") * row_span
    row_local = block_rows[0, 0] - row_base
    col_local = block_cols[0, 0] - lax.axis_index("col") * col_span
    alive = jnp.arange(slot_count, dtype=jnp.int32) < block_counts[0, 0]
    w_live = jnp.where(
        alive[:, None, None], weight_blocks[0, 0], jnp.zeros_like(weight_blocks[0, 0])
    )
    row_pick = (row_local[:, None] == jnp.arange(row_span, dtype=jnp.int32)[None, :]).astype(
        jnp.float32
    )
    col_pick = (col_local[:, None] == jnp.arange(col_span, dtype=jnp.int32)[None, :]).astype(
        jnp.float32
    )
    grad_full = lax.all_gather(out_grad, "row", axis=0, tiled=True)
    act_rows = silu_rounded(lax.all_gather(hidden_pre, "col", axis=0, tiled=True))
    count = act_rows.shape[0]
    a_stack = jnp.take(act_rows.reshape(count, row_span, width), row_local, axis=1)
    prod = jnp.einsum("nkp,kpq->nkq", a_stack, w_live, preferred_element_type=jnp.float32)
    placed = jnp.einsum("nkq,kc->ncq", prod, col_pick, precision=lax.Precision.HIGHEST)
    partial_value = placed.reshape(count, col_span * width)
    grad_rows = grad_full
    act_rows = silu_rounded(lax.all_gather(hidden_pre, "col", axis=0, tiled=True))
    count = act_rows.shape[0]
    a_stack = jnp.take(act_rows.reshape(count, row_span, width), row_local, axis=1)
    g_stack = jnp.take(grad_rows.reshape(count, col_span, width), col_local, axis=1)
    weight_grad = jnp.einsum("nkp,nkq->kpq", a_stack, g_stack, preferred_element_type=jnp.float32)
    projected = lax.psum_scatter(partial_value, "row", scatter_dimension=0, tiled=True).astype(
        jnp.bfloat16
    )
    count = hidden_pre.shape[0] * lax.axis_size("col")
    grad_rows = grad_full
    g_stack = jnp.take(grad_rows.reshape(count, col_span, width), col_local, axis=1)
    back = jnp.einsum("nkq,kpq->nkp", g_stack, w_live, preferred_element_type=jnp.float32)
    placed = jnp.einsum("nkp,kr->nrp", back, row_pick, precision=lax.Precision.HIGHEST)
    back_act = lax.psum_scatter(
        placed.reshape(count, row_span * width), "col", scatter_dimension=0, tiled=True
    )
    hidden_f = hidden_pre.astype(jnp.float32)
    sig = jax.nn.sigmoid(hidden_f)
    grad_hidden = (back_act * (sig * (1.0 + hidden_f * (1.0 - sig)))).astype(jnp.bfloat16)
    grad_blocks = jnp.where(alive[:, None, None], weight_grad, jnp.zeros_like(weight_grad))
    return (projected, grad_hidden, grad_blocks[None, None])


def solution(mesh):
    placed = (
        P("col", "row"),
        P("row", "col", None, None, None),
        P("row", "col", None),
        P("row", "col", None),
        P("row", "col"),
        P("row", "col"),
    )
    return jax.shard_map(
        on_device,
        mesh=mesh,
        in_specs=placed,
        out_specs=(P("row", "col"), P("col", "row"), P("row", "col", None, None, None)),
        check_vma=False,
    )
```

profile of v0, /device:TPU:0, one launch (start us, length us, event | category | flops | bytes accessed | tf_op | source)
XLA Modules:
  0.0 193.5 jit_solution(5066251066862516377)
XLA Ops:
  7.2 0.0 all-gather.3.cloned.1.call-start
  7.2 2.0 %copy.18 = bf16[128,2048]{0,1:T(8,128)(2,1)} copy(bf16[128,2048]{1,0:T(8,128)(2,1)} %param.8) | data formatting | bytes 1048576 | tf_op args[0]
  9.3 0.0 all-gather.3.cloned.1.call-update
  9.3 0.0 all-gather.5.cloned.1.call-start
  9.3 0.7 all-gather.5.cloned.1.call-update
  10.0 0.0 reduce-scatter.3.cloned.1.call-start
  10.7 0.7 compare_and_fusion.1
  11.4 0.7 compare_and_fusion
  12.1 36.2 %all-gather.3.cloned.1.call-done = bf16[512,2048]{0,1:T(8,128)(2,1)} async-done(((bf16[128,2048]{0,1:T(8,128)(2,1)}), bf16[512,2048]{0,1:T(8,128)(2,1)}) %all-gather.3.cloned.1.call-update) | async-done | bytes 2097168 | tf_op jit(solution)/shard_map/all_gather | solution.py:30
  48.3 4.1 %fusion.3 = bf16[512,2048]{0,1:T(8,128)(2,1)} fusion(bf16[512,2048]{0,1:T(8,128)(2,1)} %all-gather.3.cloned.1.call-done), kind=kLoop, calls=%fused_computation.7 | loop fusion | flops 6291456 | bytes 4194304 | tf_op jit(solution)/shard_map/convert_element_type | solution.py:8
  52.4 2.8 %copy.19 = bf16[512,8,256]{2,0,1:T(8,128)(2,1)S(1)} copy(bf16[512,8,256]{0,2,1:T(8,128)(2,1)} %bitcast.52) | data formatting | bytes 4194304 | tf_op jit(solution)/shard_map/reshape | solution.py:32
  55.2 0.0 copy-start.1
  55.2 2.0 %gather_fusion = bf16[8,512,256]{2,1,0:T(8,128)(2,1)} fusion(bf16[512,8,256]{2,0,1:T(8,128)(2,1)S(1)} %copy.19, s32[1024]{0:T(1024)S(1)} %pad_clamp_fusion.1), kind=kCustom, calls=%fused_computation.clone | custom fusion | bytes 4194336 | tf_op jit(solution)/shard_map/jit(_take)/gather | solution.py:32
  57.2 0.0 copy-done.1
  57.2 4.6 %convolution_bitcast_fusion.1 = f32[512,8,256]{0,2,1:T(8,128)} fusion(bf16[8,512,256]{2,1,0:T(8,128)(2,1)} %gather_fusion, pred[8]{0:T(512)(128)(4,1)S(1)} %get-tuple-element.6, bf16[1,1,8,256,256]{4,3,2,1,0:T(8,128)(2,1)S(1)} %copy-done.1, pred[8]{0:T(512)(128)(4,1)S(1)} %get-tuple-element.8), kind=kOutput, calls=%fused_computation.9 | convolution fusion | flops 538443776 | bytes 7340048 | tf_op jit(solution)/shard_map/nkp,kpq->nkq/dot_general | solution.py:33
  61.8 5.5 %copy.21 = f32[512,8,256]{2,1,0:T(8,128)} copy(f32[512,8,256]{0,2,1:T(8,128)} %convolution_bitcast_fusion.1) | data formatting | bytes 8388608 | tf_op jit(solution)/shard_map/nkp,kpq->nkq/transpose | solution.py:33
  67.3 4.3 %fusion.21 = f32[8,512,256]{2,0,1:T(8,128)S(1)} fusion(f32[512,8,256]{2,1,0:T(8,128)} %copy.21, s32[8]{0:T(128)S(1)} %get-tuple-element.5), kind=kOutput, calls=%fused_computation.33 | convolution fusion | flops 100663360 | bytes 8388640 | tf_op jit(solution)/shard_map/nkq,kc->ncq/dot_general | solution.py:34
  71.6 3.9 %copy.28 = f32[64,8,8,256]{3,1,2,0:T(8,128)} copy(f32[64,8,8,256]{3,2,1,0:T(8,128)S(1)} %bitcast.51) | data formatting | bytes 8388608
  75.5 0.0 reduce-scatter.3.cloned.1.call-update
  75.5 0.2 reduce-scatter.5.cloned.1.call-start
  75.8 3.3 %all-gather.5.cloned.1.call-done = bf16[512,2048]{1,0:T(8,128)(2,1)} async-done(((bf16[64,2048]{1,0:T(8,128)(2,1)}), bf16[512,2048]{1,0:T(8,128)(2,1)}) %all-gather.5.cloned.1.call-update) | async-done | bytes 2097168 | tf_op jit(solution)/shard_map/all_gather | solution.py:29
  79.0 3.9 %copy.22 = bf16[512,2048]{0,1:T(8,128)(2,1)} copy(bf16[512,2048]{1,0:T(8,128)(2,1)} %all-gather.5.cloned.1.call-done) | data formatting | bytes 4194304 | tf_op jit(solution)/shard_map/all_gather | solution.py:29
  82.9 2.8 %copy.23 = bf16[512,8,256]{2,0,1:T(8,128)(2,1)S(1)} copy(bf16[512,8,256]{0,2,1:T(8,128)(2,1)} %bitcast.53) | data formatting | bytes 4194304 | tf_op jit(solution)/shard_map/reshape | solution.py:47
  85.8 2.0 %gather_fusion.1 = bf16[8,512,256]{2,1,0:T(8,128)(2,1)} fusion(bf16[512,8,256]{2,0,1:T(8,128)(2,1)S(1)} %copy.23, s32[1024]{0:T(1024)S(1)} %pad_clamp_fusion), kind=kCustom, calls=%fused_computation.1.clone | custom fusion | bytes 4194336 | tf_op jit(solution)/shard_map/jit(_take)/gather | solution.py:47
  87.8 4.4 %convolution_bitcast_fusion = f32[512,8,256]{0,2,1:T(8,128)} fusion(bf16[8,512,256]{2,1,0:T(8,128)(2,1)} %gather_fusion.1, pred[8]{0:T(512)(128)(4,1)S(1)} %get-tuple-element.4, bf16[1,1,8,256,256]{4,3,2,1,0:T(8,128)(2,1)S(1)} %copy-done.1, pred[8]{0:T(512)(128)(4,1)S(1)} %get-tuple-element.8), kind=kOutput, calls=%fused_computation.8 | convolution fusion | flops 538443776 | bytes 7340048 | tf_op jit(solution)/shard_map/nkq,kpq->nkp/dot_general | solution.py:48
  92.2 5.5 %copy.24 = f32[512,8,256]{2,1,0:T(8,128)} copy(f32[512,8,256]{0,2,1:T(8,128)} %convolution_bitcast_fusion) | data formatting | bytes 8388608 | tf_op jit(solution)/shard_map/nkq,kpq->nkp/transpose | solution.py:48
  97.7 4.3 %fusion.24 = f32[8,512,256]{2,0,1:T(8,128)S(1)} fusion(f32[512,8,256]{2,1,0:T(8,128)} %copy.24, s32[8]{0:T(128)S(1)} %get-tuple-element.7), kind=kOutput, calls=%fused_computation.35 | convolution fusion | flops 100663360 | bytes 8388640 | tf_op jit(solution)/shard_map/nkp,kr->nrp/dot_general | solution.py:49
  101.9 3.9 %copy.29 = f32[64,8,8,256]{3,1,2,0:T(8,128)} copy(f32[64,8,8,256]{3,2,1,0:T(8,128)S(1)} %bitcast.50) | data formatting | bytes 8388608
  105.9 0.0 copy-start
  105.9 0.0 reduce-scatter.5.cloned.1.call-update
  105.9 1.6 copy-done
  107.5 0.0 copy-start.2
  107.5 4.0 %select_bitcast_fusion = f32[1,1,8,256,256]{4,3,2,1,0:T(8,128)} fusion(pred[8]{0:T(512)(128)(4,1)S(1)} %get-tuple-element.8, bf16[8,512,256]{2,1,0:T(8,128)(2,1)S(1)} %copy-done, pred[8]{0:T(512)(128)(4,1)S(1)} %get-tuple-element.6, bf16[8,512,256]{2,1,0:T(8,128)(2,1)} %gather_fusion.1, pred[8]{0:T(512)(128)(4,1)S(1)} %get-tuple-element.4), kind=kOutput, calls=%fused_computation.15 | convolution fusion | flops 539492352 | bytes 6291480 | tf_op jit(solution)/shard_map/nkp,nkq->kpq/dot_general | solution.py:41
  111.5 19.4 %reduce-scatter.3.cloned.1.call-done = f32[64,2048]{1,0:T(8,128)} async-done(((f32[512,2048]{1,0:T(8,128)}), f32[64,2048]{1,0:T(8,128)}) %reduce-scatter.3.cloned.1.call-update) | async-done | bytes 524304 | tf_op jit(solution)/shard_map/reduce_scatter | solution.py:42
  130.9 1.8 convert_element_type.21
  132.7 51.9 %reduce-scatter.5.cloned.1.call-done = f32[128,2048]{1,0:T(8,128)} async-done(((f32[512,2048]{1,0:T(8,128)}), f32[128,2048]{1,0:T(8,128)}) %reduce-scatter.5.cloned.1.call-update) | async-done | bytes 1048592 | tf_op jit(solution)/shard_map/reduce_scatter | solution.py:50
  184.6 0.0 copy-done.2
  184.6 2.4 %fusion.19 = bf16[128,2048]{1,0:T(8,128)(2,1)} fusion(f32[128,2048]{1,0:T(8,128)} %reduce-scatter.5.cloned.1.call-done, bf16[128,2048]{1,0:T(8,128)(2,1)S(1)} %copy-done.2), kind=kLoop, calls=%fused_computation.26 | loop fusion | flops 2621440 | bytes 2097152 | tf_op jit(solution)/shard_map/convert_element_type | solution.py:55
  (4 shorter events, 0.0 us)
Async XLA Ops:
  7.2 41.1 %all-gather.3.cloned.1.call-start = ((), (), s32[]{:S(2)}) async-start(), calls=%async_computation.2 | async-start | bytes 2621440 | tf_op jit(solution)/shard_map/all_gather | solution.py:30
  9.3 69.8 %all-gather.5.cloned.1.call-start = ((), (), s32[]{:S(2)}) async-start(), calls=%async_computation.4 | async-start | bytes 2359296 | tf_op jit(solution)/shard_map/all_gather | solution.py:29
  10.0 120.8 %reduce-scatter.3.cloned.1.call-start = ((), (), s32[]{:S(2)}) async-start(), calls=%async_computation.3 | async-start | bytes 4718592 | tf_op jit(solution)/shard_map/reduce_scatter | solution.py:42
  55.2 2.0 %copy-start.1 = (bf16[1,1,8,256,256]{4,3,2,1,0:T(8,128)(2,1)S(1)}, bf16[1,1,8,256,256]{4,3,2,1,0:T(8,128)(2,1)}, u32[]{:S(2)}) copy-start(bf16[1,1,8,256,256]{4,3,2,1,0:T(8,128)(2,1)} %param.9) | copy-start | bytes 3145732
  75.5 109.1 %reduce-scatter.5.cloned.1.call-start = ((), (), s32[]{:S(2)}) async-start(), calls=%async_computation.5 | async-start | bytes 5242880 | tf_op jit(solution)/shard_map/reduce_scatter | solution.py:50
  105.9 1.6 copy-start
  107.5 77.1 %copy-start.2 = (bf16[128,2048]{1,0:T(8,128)(2,1)S(1)}, bf16[128,2048]{1,0:T(8,128)(2,1)}, u32[]{:S(2)}) copy-start(bf16[128,2048]{1,0:T(8,128)(2,1)} %param.8) | copy-start | bytes 1572868
Sparse Core Ops, SparseCore 0:
  10.4 37.8 all-gather.2
  49.9 29.0 all-gather.4
  81.3 49.4 reduce-scatter.2
  133.7 50.8 reduce-scatter.4
where the time goes:
time: 194 us
  waiting for transfers between devices  112 us (58%)
  local copies, waits for them, and re-layouts  36 us (19%)
  matrix products  21.5 us (11%)
  between operations  14.5 us (7%)
  other arithmetic  9.6 us (5%)
    reduce_scatter x1, waiting for transfers between devices, on_device(): lax.psum_scatter(placed.reshape(count, row_span * width), 'col', scatter_...  51.9 us
    all_gather x1, waiting for transfers between devices, on_device(): lax.all_gather(hidden_pre, 'col', axis=0, tiled=True)  36.2 us
    reduce_scatter x1, waiting for transfers between devices, on_device(): lax.psum_scatter(partial_value, 'row', scatter_dimension=0, tiled=True)  19.4 us
    unnamed x9, local copies, waits for them, and re-layouts  11.5 us
    transpose x1, local copies, waits for them, and re-layouts, on_device(): jnp.einsum('nkq,kpq->nkp', g_stack, w_live, preferred_element_type=jnp.fl...  5.48 us
    transpose x1, local copies, waits for them, and re-layouts, on_device(): jnp.einsum('nkp,kpq->nkq', a_stack, w_live, preferred_element_type=jnp.fl...  5.48 us
    dot_general x1, matrix products, on_device(): jnp.einsum('nkp,kpq->nkq', a_stack, w_live, preferred_element_type=jnp.fl...  4.6 us
    dot_general x1, matrix products, on_device(): jnp.einsum('nkq,kpq->nkp', g_stack, w_live, preferred_element_type=jnp.fl...  4.39 us
  transfers between devices with their start and end apart: 4, of which 4 were waited for; matrix products, arithmetic and copies ran while one was open for 32% of the time, Pallas kernels for 0%

commit v1 on v0

--- a/solution.py
+++ b/solution.py
@@ -26,7 +26,23 @@
     col_pick = (col_local[:, None] == jnp.arange(col_span, dtype=jnp.int32)[None, :]).astype(
         jnp.float32
     )
-    grad_full = lax.all_gather(out_grad, "row", axis=0, tiled=True)
+    g_now, passed, ready = (lax.axis_size("row"), lax.axis_index("row"), out_grad.shape[0])
+    cards = [(tick, (tick + 1) % g_now) for tick in range(g_now)]
+    rack = [(tick, (tick - 1) % g_now) for tick in range(g_now)]
+    grad_full = jnp.zeros((*out_grad.shape[:0], g_now * ready, *out_grad.shape[1:]), out_grad.dtype)
+    grad_full = lax.dynamic_update_slice_in_dim(grad_full, out_grad, passed * ready, axis=0)
+    block_next = arr_now = out_grad
+    y = g_now // 2
+    for m in tuple(range(1, y + 1)):
+        block_next = lax.ppermute(block_next, "row", cards)
+        grad_full = lax.dynamic_update_slice_in_dim(
+            grad_full, block_next, (passed - m) % g_now * ready, axis=0
+        )
+        if m < g_now - y:
+            arr_now = lax.ppermute(arr_now, "row", rack)
+            grad_full = lax.dynamic_update_slice_in_dim(
+                grad_full, arr_now, (passed + m) % g_now * ready, axis=0
+            )
     act_rows = silu_rounded(lax.all_gather(hidden_pre, "col", axis=0, tiled=True))
     count = act_rows.shape[0]
     a_stack = jnp.take(act_rows.reshape(count, row_span, width), row_local, axis=1)

time: 194 us -> 230 us (1.19)
  local copies, waits for them, and re-layouts: 36 us -> 69.3 us
  starting transfers between devices: 0.34 us -> 12.5 us
  waiting for transfers between devices: 112 us -> 104 us
    all_gather x1, waiting for transfers between devices: 36.2 us -> 0.02 us  [on_device(): lax.all_gather(hidden_pre, 'col', axis=0, tiled=True)]
    dynamic_update_slice x0 -> x8, local copies, waits for them, and re-layouts: none -> 35.6 us  [the longest x3 16.8 us: on_device(): lax.dynamic_update_slice_in_dim(grad_full, arr_now, (passed + m) % g_now...]
    reduce_scatter x1, waiting for transfers between devices: 19.4 us -> 50 us  [on_device(): lax.psum_scatter(partial_value, 'row', scatter_dimension=0, tiled=True)]
    ppermute x0 -> x7, waiting for transfers between devices: none -> 25.3 us  [the longest x4 23.5 us: on_device(): block_next = lax.ppermute(block_next, 'row', cards)]
    reduce_scatter x1, waiting for transfers between devices: 51.9 us -> 29 us  [on_device(): lax.psum_scatter(placed.reshape(count, row_span * width), 'col', scatter_...]
    ppermute x0 -> x7, starting transfers between devices: none -> 12.2 us  [the longest x3 11.7 us: on_device(): arr_now = lax.ppermute(arr_now, 'row', rack)]
    all_gather x1 -> x0, local copies, waits for them, and re-layouts: 3.91 us -> none  [on_device(): grad_full = lax.all_gather(out_grad, 'row', axis=0, tiled=True)]
    all_gather x1 -> x0, waiting for transfers between devices: 3.26 us -> none  [on_device(): grad_full = lax.all_gather(out_grad, 'row', axis=0, tiled=True)]
  transfers between devices with their start and end apart: 4 -> 10, of which waited for: 4 -> 7; matrix products, arithmetic and copies ran while one was open for 32% -> 40% of each run, Pallas kernels for 0% -> 0%
where the time goes in v1:
time: 230 us; the launch traced here: 229 us
  waiting for transfers between devices  104 us (45%)
  local copies, waits for them, and re-layouts  69.3 us (30%)
  matrix products  19.6 us (9%)
  between operations  14.8 us (6%)
  starting transfers between devices  12.5 us (5%)
  other arithmetic  8.29 us (4%)
    reduce_scatter x1, waiting for transfers between devices, on_device(): lax.psum_scatter(partial_value, 'row', scatter_dimension=0, tiled=True)  50 us
    reduce_scatter x1, waiting for transfers between devices, on_device(): lax.psum_scatter(placed.reshape(count, row_span * width), 'col', scatter_...  29 us
    ppermute x4, waiting for transfers between devices, on_device(): block_next = lax.ppermute(block_next, 'row', cards)  23.5 us
    dynamic_update_slice x3, local copies, waits for them, and re-layouts, on_device(): lax.dynamic_update_slice_in_dim(grad_full, arr_now, (passed + m) % g_now...  16.8 us
    dynamic_update_slice x4, local copies, waits for them, and re-layouts, on_device(): lax.dynamic_update_slice_in_dim(grad_full, block_next, (passed - m) % g_n...  16.4 us
    unnamed x22, local copies, waits for them, and re-layouts  12.9 us
    ppermute x3, starting transfers between devices, on_device(): arr_now = lax.ppermute(arr_now, 'row', rack)  11.7 us
    transpose x1, local copies, waits for them, and re-layouts, on_device(): jnp.einsum('nkp,kpq->nkq', a_stack, w_live, preferred_element_type=jnp.fl...  5.53 us
  transfers between devices with their start and end apart: 10, of which 7 were waited for; matrix products, arithmetic and copies ran while one was open for 40% of the time, Pallas kernels for 0%

profile of v1, /device:TPU:0, one launch (start us, length us, event | category | flops | bytes accessed | tf_op | source)
XLA Modules:
  0.0 228.9 jit_solution(7013939721395687357)
XLA Ops:
  7.2 0.0 all-gather.2.cloned.1.call-start
  7.2 2.0 copy.10
  9.3 0.0 all-gather.2.cloned.1.call-update
  9.3 0.0 copy-start.8
  9.3 0.0 reduce-scatter.5.cloned.1.call-start
  9.3 1.2 copy.14
  10.6 0.5 collective-permute-start
  11.1 4.1 %collective-permute-start.1 = (bf16[64,2048]{0,1:T(8,128)(2,1)S(1)}, bf16[64,2048]{0,1:T(8,128)(2,1)S(1)}, u32[]{:S(2)}, u32[]{:S(2)}) collective-permute-start(bf16[64,2048]{0,1:T(8,128)(2,1)S(1)} %copy.14), channel_id=1, source_target_pairs={{0,28},{4,0},{8,4},{12,8},{16,12},{20,16},{24,20},{28,24},{1,29},{... | collective-permute-start | bytes 786440 | tf_op jit(solution)/shard_map/ppermute | solution.py:42
  15.2 9.8 %collective-permute-done = bf16[64,2048]{0,1:T(8,128)(2,1)S(1)} collective-permute-done((bf16[64,2048]{0,1:T(8,128)(2,1)S(1)}, bf16[64,2048]{0,1:T(8,128)(2,1)S(1)}, u32[]{:S(2)}, u32[]{:S(2)}) %collective-permute-start) | collective-permute-done | bytes 262176 | tf_op jit(solution)/shard_map/ppermute | solution.py:37
  24.9 0.5 collective-permute-done.1
  25.4 3.8 %collective-permute-start.3 = (bf16[64,2048]{0,1:T(8,128)(2,1)S(1)}, bf16[64,2048]{0,1:T(8,128)(2,1)}, u32[]{:S(2)}, u32[]{:S(2)}) collective-permute-start(bf16[64,2048]{0,1:T(8,128)(2,1)S(1)} %collective-permute-done.1), channel_id=1, source_target_pairs={{0,28},{4,0},{8,4},{12,8},{16,12},{20,16},{24,20},{28,24},{1,29},{... | collective-permute-start | bytes 786440 | tf_op jit(solution)/shard_map/ppermute | solution.py:42
  29.3 8.2 %collective-permute-done.2 = bf16[64,2048]{0,1:T(8,128)(2,1)S(1)} collective-permute-done((bf16[64,2048]{0,1:T(8,128)(2,1)S(1)}, bf16[64,2048]{0,1:T(8,128)(2,1)S(1)}, u32[]{:S(2)}, u32[]{:S(2)}) %collective-permute-start.2) | collective-permute-done | bytes 262176 | tf_op jit(solution)/shard_map/ppermute | solution.py:37
  37.5 1.2 collective-permute-done.3
  38.7 3.8 %collective-permute-start.5 = (bf16[64,2048]{0,1:T(8,128)(2,1)}, bf16[64,2048]{0,1:T(8,128)(2,1)}, u32[]{:S(2)}, u32[]{:S(2)}) collective-permute-start(bf16[64,2048]{0,1:T(8,128)(2,1)} %collective-permute-done.3), channel_id=1, source_target_pairs={{0,28},{4,0},{8,4},{12,8},{16,12},{20,16},{24,20},{28,24},{1,29},{... | collective-permute-start | bytes 786440 | tf_op jit(solution)/shard_map/ppermute | solution.py:42
  42.5 5.6 %collective-permute-done.4 = bf16[64,2048]{0,1:T(8,128)(2,1)} collective-permute-done((bf16[64,2048]{0,1:T(8,128)(2,1)S(1)}, bf16[64,2048]{0,1:T(8,128)(2,1)}, u32[]{:S(2)}, u32[]{:S(2)}) %collective-permute-start.4) | collective-permute-done | bytes 262176 | tf_op jit(solution)/shard_map/ppermute | solution.py:37
  48.1 0.0 collective-permute-start.6
  48.9 0.1 broadcast_in_dim.43
  49.1 2.4 %dynamic_update_slice.24 = bf16[512,2048]{0,1:T(8,128)(2,1)S(1)} dynamic-update-slice(bf16[512,2048]{0,1:T(8,128)(2,1)S(1)} %broadcast_in_dim.43, bf16[64,2048]{0,1:T(8,128)(2,1)S(1)} %copy.14, s32[]{:T(128)S(6)} %select_n.71, s32[]{:T(128)} %constant.75.clone.1) | dynamic-update-slice | bytes 524292 | tf_op jit(solution)/shard_map/dynamic_update_slice | solution.py:33
  51.5 3.6 %dynamic_update_slice.25 = bf16[512,2048]{0,1:T(8,128)(2,1)S(1)} dynamic-update-slice(bf16[512,2048]{0,1:T(8,128)(2,1)S(1)} %dynamic_update_slice.24, bf16[64,2048]{0,1:T(8,128)(2,1)S(1)} %collective-permute-done, s32[]{:T(128)S(6)} %select_n.73, s32[]{:T(128)} %constant.75.clone.1) | dynamic-update-slice | bytes 524292 | tf_op jit(solution)/shard_map/dynamic_update_slice | solution.py:38
  55.2 5.9 %dynamic_update_slice.26 = bf16[512,2048]{0,1:T(8,128)(2,1)S(1)} dynamic-update-slice(bf16[512,2048]{0,1:T(8,128)(2,1)S(1)} %dynamic_update_slice.25, bf16[64,2048]{0,1:T(8,128)(2,1)} %copy-done.4, s32[]{:T(128)S(6)} %select_n.75, s32[]{:T(128)} %constant.75.clone.1) | dynamic-update-slice | bytes 524292 | tf_op jit(solution)/shard_map/dynamic_update_slice | solution.py:43
  61.1 2.0 dynamic_update_slice.27
  63.1 4.9 %dynamic_update_slice.28 = bf16[512,2048]{0,1:T(8,128)(2,1)S(1)} dynamic-update-slice(bf16[512,2048]{0,1:T(8,128)(2,1)S(1)} %dynamic_update_slice.27, bf16[64,2048]{0,1:T(8,128)(2,1)} %collective-permute-done.3, s32[]{:T(128)S(6)} %select_n.79, s32[]{:T(128)} %constant.75.clone.1) | dynamic-update-slice | bytes 524292 | tf_op jit(solution)/shard_map/dynamic_update_slice | solution.py:43
  68.0 5.9 %dynamic_update_slice.29 = bf16[512,2048]{0,1:T(8,128)(2,1)S(1)} dynamic-update-slice(bf16[512,2048]{0,1:T(8,128)(2,1)S(1)} %dynamic_update_slice.28, bf16[64,2048]{0,1:T(8,128)(2,1)} %collective-permute-done.4, s32[]{:T(128)S(6)} %select_n.81, s32[]{:T(128)} %constant.75.clone.1) | dynamic-update-slice | bytes 524292 | tf_op jit(solution)/shard_map/dynamic_update_slice | solution.py:38
  74.0 5.9 %dynamic_update_slice.30 = bf16[512,2048]{0,1:T(8,128)(2,1)S(1)} dynamic-update-slice(bf16[512,2048]{0,1:T(8,128)(2,1)S(1)} %dynamic_update_slice.29, bf16[64,2048]{0,1:T(8,128)(2,1)} %collective-permute-done.5, s32[]{:T(128)S(6)} %select_n.83, s32[]{:T(128)} %constant.75.clone.1) | dynamic-update-slice | bytes 524292 | tf_op jit(solution)/shard_map/dynamic_update_slice | solution.py:43
  79.9 4.9 %dynamic_update_slice.31 = bf16[512,2048]{0,1:T(8,128)(2,1)S(1)} dynamic-update-slice(bf16[512,2048]{0,1:T(8,128)(2,1)S(1)} %dynamic_update_slice.30, bf16[64,2048]{0,1:T(8,128)(2,1)} %collective-permute-done.6, s32[]{:T(128)S(6)} %select_n.85, s32[]{:T(128)} %constant.75.clone.1) | dynamic-update-slice | bytes 524292 | tf_op jit(solution)/shard_map/dynamic_update_slice | solution.py:38
  84.8 2.4 %copy.17 = bf16[512,8,256]{2,0,1:T(8,128)(2,1)} copy(bf16[512,8,256]{0,2,1:T(8,128)(2,1)S(1)} %bitcast.52) | data formatting | bytes 4194304 | tf_op jit(solution)/shard_map/reshape | solution.py:63
  87.2 2.4 %gather_fusion.1 = bf16[8,512,256]{2,1,0:T(8,128)(2,1)S(1)} fusion(bf16[512,8,256]{2,0,1:T(8,128)(2,1)} %copy.17, s32[1024]{0:T(1024)S(1)} %pad_clamp_fusion), kind=kCustom, calls=%fused_computation.1.clone | custom fusion | bytes 4194336 | tf_op jit(solution)/shard_map/jit(_take)/gather | solution.py:63
  89.6 2.8 %convolution_bitcast_fusion = f32[512,8,256]{0,2,1:T(8,128)} fusion(bf16[8,512,256]{2,1,0:T(8,128)(2,1)S(1)} %gather_fusion.1, pred[8]{0:T(512)(128)(4,1)S(1)} %get-tuple-element.4, bf16[1,1,8,256,256]{4,3,2,1,0:T(8,128)(2,1)S(1)} %copy-done.2, pred[8]{0:T(512)(128)(4,1)S(1)} %get-tuple-element.8), kind=kOutput, calls=%fused_computation.8 | convolution fusion | flops 538443776 | bytes 7340048 | tf_op jit(solution)/shard_map/nkq,kpq->nkp/dot_general | solution.py:64
  92.4 5.5 %copy.18 = f32[512,8,256]{2,1,0:T(8,128)} copy(f32[512,8,256]{0,2,1:T(8,128)} %convolution_bitcast_fusion) | data formatting | bytes 8388608 | tf_op jit(solution)/shard_map/nkq,kpq->nkp/transpose | solution.py:64
  97.9 4.2 %fusion.24 = f32[8,512,256]{2,0,1:T(8,128)S(1)} fusion(f32[512,8,256]{2,1,0:T(8,128)} %copy.18, s32[8]{0:T(128)S(1)} %get-tuple-element.7), kind=kOutput, calls=%fused_computation.35 | convolution fusion | flops 100663360 | bytes 8388640 | tf_op jit(solution)/shard_map/nkp,kr->nrp/dot_general | solution.py:65
  102.1 3.9 %copy.23 = f32[64,8,8,256]{3,1,2,0:T(8,128)} copy(f32[64,8,8,256]{3,2,1,0:T(8,128)S(1)} %bitcast.51) | data formatting | bytes 8388608
  106.0 0.0 reduce-scatter.5.cloned.1.call-update
  106.0 0.2 reduce-scatter.3.cloned.1.call-start
  106.3 0.0 all-gather.2.cloned.1.call-done
  106.3 4.1 %fusion.3 = bf16[512,2048]{0,1:T(8,128)(2,1)} fusion(bf16[512,2048]{0,1:T(8,128)(2,1)} %all-gather.2.cloned.1.call-done), kind=kLoop, calls=%fused_computation.7 | loop fusion | flops 6291456 | bytes 4194304 | tf_op jit(solution)/shard_map/convert_element_type | solution.py:8
  110.4 2.8 %copy.11 = bf16[512,8,256]{2,0,1:T(8,128)(2,1)S(1)} copy(bf16[512,8,256]{0,2,1:T(8,128)(2,1)} %bitcast.53) | data formatting | bytes 4194304 | tf_op jit(solution)/shard_map/reshape | solution.py:48
  113.2 2.0 gather_fusion
  115.2 4.5 %convolution_bitcast_fusion.1 = f32[512,8,256]{0,2,1:T(8,128)} fusion(bf16[8,512,256]{2,1,0:T(8,128)(2,1)} %gather_fusion, pred[8]{0:T(512)(128)(4,1)S(1)} %get-tuple-element.6, bf16[1,1,8,256,256]{4,3,2,1,0:T(8,128)(2,1)S(1)} %copy-done.2, pred[8]{0:T(512)(128)(4,1)S(1)} %get-tuple-element.8), kind=kOutput, calls=%fused_computation.9 | convolution fusion | flops 538443776 | bytes 7340048 | tf_op jit(solution)/shard_map/nkp,kpq->nkq/dot_general | solution.py:49
  119.7 5.5 %copy.13 = f32[512,8,256]{2,1,0:T(8,128)} copy(f32[512,8,256]{0,2,1:T(8,128)} %convolution_bitcast_fusion.1) | data formatting | bytes 8388608 | tf_op jit(solution)/shard_map/nkp,kpq->nkq/transpose | solution.py:49
  125.2 4.2 %fusion.21 = f32[8,512,256]{2,0,1:T(8,128)S(1)} fusion(f32[512,8,256]{2,1,0:T(8,128)} %copy.13, s32[8]{0:T(128)S(1)} %get-tuple-element.5), kind=kOutput, calls=%fused_computation.33 | convolution fusion | flops 100663360 | bytes 8388640 | tf_op jit(solution)/shard_map/nkq,kc->ncq/dot_general | solution.py:50
  129.5 3.9 %copy.22 = f32[64,8,8,256]{3,1,2,0:T(8,128)} copy(f32[64,8,8,256]{3,2,1,0:T(8,128)S(1)} %bitcast.50) | data formatting | bytes 8388608
  133.4 0.0 reduce-scatter.3.cloned.1.call-update
  133.4 1.8 copy-done.1
  135.2 4.0 %select_bitcast_fusion = f32[1,1,8,256,256]{4,3,2,1,0:T(8,128)} fusion(pred[8]{0:T(512)(128)(4,1)S(1)} %get-tuple-element.8, bf16[8,512,256]{2,1,0:T(8,128)(2,1)} %gather_fusion, pred[8]{0:T(512)(128)(4,1)S(1)} %get-tuple-element.6, bf16[8,512,256]{2,1,0:T(8,128)(2,1)S(1)} %copy-done.1, pred[8]{0:T(512)(128)(4,1)S(1)} %get-tuple-element.4), kind=kOutput, calls=%fused_computation.15 | convolution fusion | flops 539492352 | bytes 6291480 | tf_op jit(solution)/shard_map/nkp,nkq->kpq/dot_general | solution.py:57
  139.2 29.0 %reduce-scatter.5.cloned.1.call-done = f32[128,2048]{1,0:T(8,128)} async-done(((f32[512,2048]{1,0:T(8,128)}), f32[128,2048]{1,0:T(8,128)}) %reduce-scatter.5.cloned.1.call-update) | async-done | bytes 1048592 | tf_op jit(solution)/shard_map/reduce_scatter | solution.py:66
  168.2 2.4 %fusion.19 = bf16[128,2048]{1,0:T(8,128)(2,1)} fusion(f32[128,2048]{1,0:T(8,128)} %reduce-scatter.5.cloned.1.call-done, bf16[128,2048]{1,0:T(8,128)(2,1)S(1)} %copy-done.3), kind=kLoop, calls=%fused_computation.26 | loop fusion | flops 2621440 | bytes 2097152 | tf_op jit(solution)/shard_map/convert_element_type | solution.py:71
  170.6 50.0 %reduce-scatter.3.cloned.1.call-done = f32[64,2048]{1,0:T(8,128)} async-done(((f32[512,2048]{1,0:T(8,128)}), f32[64,2048]{1,0:T(8,128)}) %reduce-scatter.3.cloned.1.call-update) | async-done | bytes 524304 | tf_op jit(solution)/shard_map/reduce_scatter | solution.py:58
  220.6 1.8 convert_element_type.21
  (26 shorter events, 0.1 us)
Async XLA Ops:
  7.2 30.3 %copy-start.7 = (s32[1,1,8]{2,1,0:T(1,128)S(1)}, s32[1,1,8]{2,1,0:T(1,128)}, u32[]{:S(2)}) copy-start(s32[1,1,8]{2,1,0:T(1,128)} %param.11) | copy-start | bytes 100
  7.2 99.1 %all-gather.2.cloned.1.call-start = ((), (), s32[]{:S(2)}) async-start(), calls=%async_computation.2 | async-start | bytes 2621440 | tf_op jit(solution)/shard_map/all_gather | solution.py:46
  9.3 42.2 %copy-start.8 = (s32[1,1,8]{2,1,0:T(1,128)S(1)}, s32[1,1,8]{2,1,0:T(1,128)}, u32[]{:S(2)}) copy-start(s32[1,1,8]{2,1,0:T(1,128)} %param.10) | copy-start | bytes 100
  9.3 158.9 %reduce-scatter.5.cloned.1.call-start = ((), (), s32[]{:S(2)}) async-start(), calls=%async_computation.4 | async-start | bytes 5242880 | tf_op jit(solution)/shard_map/reduce_scatter | solution.py:66
  10.6 14.4 %collective-permute-start = (bf16[64,2048]{0,1:T(8,128)(2,1)S(1)}, bf16[64,2048]{0,1:T(8,128)(2,1)S(1)}, u32[]{:S(2)}, u32[]{:S(2)}) collective-permute-start(bf16[64,2048]{0,1:T(8,128)(2,1)S(1)} %copy.14), channel_id=1, source_target_pairs={{0,4},{4,8},{8,12},{12,16},{16,20},{20,24},{24,28},{28,0},{1,5},{5... | collective-permute-start | bytes 786440 | tf_op jit(solution)/shard_map/ppermute | solution.py:37
  11.1 14.4 %collective-permute-start.1 = (bf16[64,2048]{0,1:T(8,128)(2,1)S(1)}, bf16[64,2048]{0,1:T(8,128)(2,1)S(1)}, u32[]{:S(2)}, u32[]{:S(2)}) collective-permute-start(bf16[64,2048]{0,1:T(8,128)(2,1)S(1)} %copy.14), channel_id=1, source_target_pairs={{0,28},{4,0},{8,4},{12,8},{16,12},{20,16},{24,20},{28,24},{1,29},{... | collective-permute-start | bytes 786440 | tf_op jit(solution)/shard_map/ppermute | solution.py:42
  24.9 12.5 %collective-permute-start.2 = (bf16[64,2048]{0,1:T(8,128)(2,1)S(1)}, bf16[64,2048]{0,1:T(8,128)(2,1)S(1)}, u32[]{:S(2)}, u32[]{:S(2)}) collective-permute-start(bf16[64,2048]{0,1:T(8,128)(2,1)S(1)} %collective-permute-done), channel_id=1, source_target_pairs={{0,4},{4,8},{8,12},{12,16},{16,20},{20,24},{24,28},{28,0},{1,5},{5... | collective-permute-start | bytes 786440 | tf_op jit(solution)/shard_map/ppermute | solution.py:37
  25.4 23.5 %copy-start.4 = (bf16[64,2048]{0,1:T(8,128)(2,1)}, bf16[64,2048]{0,1:T(8,128)(2,1)S(1)}, u32[]{:S(2)}) copy-start(bf16[64,2048]{0,1:T(8,128)(2,1)S(1)} %collective-permute-done.1) | copy-start | bytes 786436
  25.4 13.2 %collective-permute-start.3 = (bf16[64,2048]{0,1:T(8,128)(2,1)S(1)}, bf16[64,2048]{0,1:T(8,128)(2,1)}, u32[]{:S(2)}, u32[]{:S(2)}) collective-permute-start(bf16[64,2048]{0,1:T(8,128)(2,1)S(1)} %collective-permute-done.1), channel_id=1, source_target_pairs={{0,28},{4,0},{8,4},{12,8},{16,12},{20,16},{24,20},{28,24},{1,29},{... | collective-permute-start | bytes 786440 | tf_op jit(solution)/shard_map/ppermute | solution.py:42
  37.4 11.5 %copy-start.5 = (bf16[64,2048]{0,1:T(8,128)(2,1)}, bf16[64,2048]{0,1:T(8,128)(2,1)S(1)}, u32[]{:S(2)}) copy-start(bf16[64,2048]{0,1:T(8,128)(2,1)S(1)} %collective-permute-done.2) | copy-start | bytes 786436
  37.4 10.7 %collective-permute-start.4 = (bf16[64,2048]{0,1:T(8,128)(2,1)S(1)}, bf16[64,2048]{0,1:T(8,128)(2,1)}, u32[]{:S(2)}, u32[]{:S(2)}) collective-permute-start(bf16[64,2048]{0,1:T(8,128)(2,1)S(1)} %collective-permute-done.2), channel_id=1, source_target_pairs={{0,4},{4,8},{8,12},{12,16},{16,20},{20,24},{24,28},{28,0},{1,5},{5... | collective-permute-start | bytes 786440 | tf_op jit(solution)/shard_map/ppermute | solution.py:37
  38.7 35.3 %collective-permute-start.5 = (bf16[64,2048]{0,1:T(8,128)(2,1)}, bf16[64,2048]{0,1:T(8,128)(2,1)}, u32[]{:S(2)}, u32[]{:S(2)}) collective-permute-start(bf16[64,2048]{0,1:T(8,128)(2,1)} %collective-permute-done.3), channel_id=1, source_target_pairs={{0,28},{4,0},{8,4},{12,8},{16,12},{20,16},{24,20},{28,24},{1,29},{... | collective-permute-start | bytes 786440 | tf_op jit(solution)/shard_map/ppermute | solution.py:42
  48.1 31.8 %collective-permute-start.6 = (bf16[64,2048]{0,1:T(8,128)(2,1)}, bf16[64,2048]{0,1:T(8,128)(2,1)}, u32[]{:S(2)}, u32[]{:S(2)}) collective-permute-start(bf16[64,2048]{0,1:T(8,128)(2,1)} %collective-permute-done.4), channel_id=1, source_target_pairs={{0,4},{4,8},{8,12},{12,16},{16,20},{20,24},{24,28},{28,0},{1,5},{5... | collective-permute-start | bytes 786440 | tf_op jit(solution)/shard_map/ppermute | solution.py:37
  51.4 9.7 %copy-start.6 = (bf16[64,2048]{0,1:T(8,128)(2,1)S(1)}, bf16[64,2048]{0,1:T(8,128)(2,1)}, u32[]{:S(2)}) copy-start(bf16[64,2048]{0,1:T(8,128)(2,1)} %copy-done.5) | copy-start | bytes 786436
  87.2 2.4 %copy-start.2 = (bf16[1,1,8,256,256]{4,3,2,1,0:T(8,128)(2,1)S(1)}, bf16[1,1,8,256,256]{4,3,2,1,0:T(8,128)(2,1)}, u32[]{:S(2)}) copy-start(bf16[1,1,8,256,256]{4,3,2,1,0:T(8,128)(2,1)} %param.9) | copy-start | bytes 3145732
  89.6 2.8 %copy-start = (bf16[8,512,256]{2,1,0:T(8,128)(2,1)}, bf16[8,512,256]{2,1,0:T(8,128)(2,1)S(1)}, u32[]{:S(2)}) copy-start(bf16[8,512,256]{2,1,0:T(8,128)(2,1)S(1)} %gather_fusion.1) | copy-start | bytes 6291460
  106.0 114.5 %reduce-scatter.3.cloned.1.call-start = ((), (), s32[]{:S(2)}) async-start(), calls=%async_computation.3 | async-start | bytes 4718592 | tf_op jit(solution)/shard_map/reduce_scatter | solution.py:58
  133.4 1.8 copy-start.1
  135.2 32.9 %copy-start.3 = (bf16[128,2048]{1,0:T(8,128)(2,1)S(1)}, bf16[128,2048]{1,0:T(8,128)(2,1)}, u32[]{:S(2)}) copy-start(bf16[128,2048]{1,0:T(8,128)(2,1)} %param.8) | copy-start | bytes 1572868
Sparse Core Ops, SparseCore 0:
  10.4 37.8 all-gather.1
  106.2 61.9 reduce-scatter.4
  170.6 49.9 reduce-scatter.2
